TPU v7x, 32 devices: a whole 2x2x4 slice. The times are simulated.
32 devices in a mesh: tile: 8 (over z, x), pos: 4 (over y, core).
Axes of the slice: x: 2, y: 2, z: 4, core: 2. Of those that a mesh axis runs over, the one named last changes fastest.
Arguments:
- probe_field: float32 [2, 256, 256], replicated, may hold values from -6 to 6
- specimen: bfloat16 [2, 2, 4096, 512], P(None, None, 'tile'), may hold values from -6 to 6
- amplitude: bfloat16 [256, 256, 256], P(('tile', 'pos')), may hold values from 0 to 2
- scan_anchor: int32 [256, 2], P(('tile', 'pos')), may hold values from 0 to 3840, as said below
- counts: int32 [32], P(('tile', 'pos')), may hold values from 2 to 8, as said below
Outputs:
- object_grad: float32 [2, 2, 4096, 512], P(None, None, 'tile')
- probe_grad: float32 [2, 256, 256], replicated
Inputs may be any that keep to these rules, and one draw needn't show every extreme that they name: `scan_anchor`: slot q's patch row r lies in the tile of index t = q // 32: t * 512 <= r < (t + 1) * 512, and the patch lies inside the object. Live slots of a device are its first counts slots; some device is full in every draw.
All inputs are finite; a program needn't handle non-finite values.
Results may differ from a plain program's by a relative error of at most 0.012.
Values may be sent and summed in bfloat16 or wider, within the bound.
No kernel may reach another device: no remote copies, remote signals or barrier semaphores. Data moves between devices by JAX's collectives and lax.ppermute only.
A program may use at most 64 MiB of HBM per device.

v0:
```python
import math

import jax
import jax.numpy as jnp
import ml_dtypes
import numpy as np
from jax import lax
from jax.experimental import pallas as pl
from jax.experimental.pallas import tpu as pltpu
from jax.sharding import PartitionSpec as P

PROP_COEF = 0.5
AMP_EPS = 0.05
LANES = 128
CHUNK = 32
EARLY = 4
MIDDLE = 4


def fixed_tables(edge):
    index = np.arange(edge)
    angles = (np.outer(index, index) % edge) * (2.0 * math.pi / edge)
    cosine = (np.cos(angles) / math.sqrt(edge)).astype(ml_dtypes.bfloat16).astype(np.float64)
    sine = (np.sin(angles) / math.sqrt(edge)).astype(ml_dtypes.bfloat16).astype(np.float64)
    forward = cosine - 1j * sine
    centred = np.where(index < edge // 2, index, index - edge)
    ramp = np.exp(-1j * (PROP_COEF * math.pi / edge) * centred * centred)
    spread = (np.conj(forward) * ramp[None, :]) @ forward
    planes = [
        plane for matrix in (spread, forward) for plane in (matrix.real, matrix.imag, -matrix.imag)
    ]
    return jnp.asarray(np.stack(planes).astype(ml_dtypes.bfloat16))


def lay_tables(planes, tables):
    edge = planes.shape[1]
    lo, hi = pl.ds(0, edge), pl.ds(edge, edge)
    for k in range(2):
        real, imag, negated = (planes[3 * k + i] for i in range(3))
        left, right = tables[2 * k : 2 * k + 2]
        left[lo, lo], left[lo, hi], left[hi, lo], left[hi, hi] = real, negated, imag, real
        right[lo, lo], right[lo, hi], right[hi, lo], right[hi, hi] = real, imag, negated, real


def interleaved(first, second):
    marks = [(k / len(first), 0, k) for k in range(len(first))]
    marks += [((k + 0.5) / len(second), 1, k) for k in range(len(second))]
    for _, which, k in sorted(marks):
        (first, second)[which][k]()


def slot_stages(slot, alive, base_row, refs, work):
    corner, probe, amp, tables, wide, acc, probe_acc = refs
    rolled, arriving, field, stack, joined = work
    left_a, right_a, left_f, right_f = tables
    edge = probe.shape[1]
    col_tiles = wide.shape[2]
    parts = edge // LANES
    lane = lax.broadcasted_iota(jnp.int32, (CHUNK, LANES), 1)
    row = corner[slot, 0] - base_row
    col = corner[slot, 1]
    first = jnp.minimum(col // LANES, col_tiles - parts - 1)
    shift = col - first * LANES
    turn = jnp.where(shift >= LANES, 0, shift)
    back = jnp.where(turn == 0, 0, LANES - turn)
    own = lane >= shift
    near = lane < LANES - shift

    def patch(part, s, i, j):
        rows = pl.ds(row + i, CHUNK)
        main = wide[part, s, first + j, rows, :]
        if j > 0:
            return main
        return jnp.where(own, main, wide[part, s, first + parts, rows, :])

    def place(part, s, i, j, value):
        rows = pl.ds(row + i, CHUNK)
        if j > 0:
            acc[part, s, first + j, rows, :] += value
        else:
            acc[part, s, first, rows, :] += jnp.where(own, value, 0.0)
            acc[part, s, first + parts, rows, :] += jnp.where(own, 0.0, value)

    def put(i, j, re, im):
        cols = pl.ds(j * LANES, LANES)
        stack[pl.ds(i, CHUNK), cols] = re.astype(jnp.bfloat16)
        stack[pl.ds(edge + i, CHUNK), cols] = im.astype(jnp.bfloat16)

    def halves():
        return [(j, pl.ds(j * LANES, LANES)) for j in range(parts)]

    def enter(i):
        rows = pl.ds(i, CHUNK)
        turned = [
            [pltpu.roll(probe[part, rows, cols], turn, 1) for j, cols in halves()]
            for part in range(2)
        ]
        for j, cols in halves():
            u_re, u_im = [
                jnp.where(own, turned[part][j], turned[part][j - 1]) for part in range(2)
            ]
            rolled[0, rows, cols] = u_re
            rolled[1, rows, cols] = u_im
            o_re, o_im = patch(0, 0, i, j), patch(1, 0, i, j)
            put(i, j, u_re * o_re - u_im * o_im, u_re * o_im + u_im * o_re)

    def second_slice(i):
        rows = pl.ds(i, CHUNK)
        for j, cols in halves():
            u_re, u_im = arriving[0, rows, cols], arriving[1, rows, cols]
            o_re, o_im = patch(0, 1, i, j), patch(1, 1, i, j)
            put(i, j, u_re * o_re - u_im * o_im, u_re * o_im + u_im * o_re)

    def residual(i):
        rows = pl.ds(i, CHUNK)
        for j, cols in halves():
            far_re, far_im = field[0, rows, cols], field[1, rows, cols]
            measured = amp[slot, rows, cols].astype(jnp.float32) * alive
            ratio = measured * lax.rsqrt(far_re * far_re + far_im * far_im + AMP_EPS)
            put(i, j, (alive - ratio) * far_re, (ratio - alive) * far_im)

    def second_grad(i):
        rows = pl.ds(i, CHUNK)
        for j, cols in halves():
            u_re, u_im = arriving[0, rows, cols], arriving[1, rows, cols]
            w_re, w_im = field[0, rows, cols], field[1, rows, cols]
            place(0, 1, i, j, u_re * w_re - u_im * w_im)
            place(1, 1, i, j, u_re * w_im + u_im * w_re)
            o_re, o_im = patch(0, 1, i, j), patch(1, 1, i, j)
            put(i, j, o_re * w_re - o_im * w_im, o_re * w_im + o_im * w_re)

    def first_grad(i):
        rows = pl.ds(i, CHUNK)
        turned = [[None] * parts for _ in range(2)]
        for j, cols in halves():
            u_re, u_im = rolled[0, rows, cols], rolled[1, rows, cols]
            w_re, w_im = field[0, rows, cols], field[1, rows, cols]
            place(0, 0, i, j, u_re * w_re - u_im * w_im)
            place(1, 0, i, j, u_re * w_im + u_im * w_re)
            o_re, o_im = patch(0, 0, i, j), patch(1, 0, i, j)
            turned[0][j] = pltpu.roll(o_re * w_re - o_im * w_im, back, 1)
            turned[1][j] = pltpu.roll(o_re * w_im + o_im * w_re, back, 1)
        for part in range(2):
            for j, cols in halves():
                after = turned[part][(j + 1) % parts]
                probe_acc[part, rows, cols] += jnp.where(near, turned[part][j], after)

    def two_sided(left, right, out):
        def rows_of(part):
            span = pl.ds(part * edge, edge)
            joined[:, span] = jnp.dot(
                left[span, :], stack[...], preferred_element_type=jnp.float32
            ).astype(jnp.bfloat16)

        def cols_of(part):
            out[part] = jnp.dot(
                joined[...],
                right[:, pl.ds(part * edge, edge)],
                preferred_element_type=jnp.float32,
            )

        return [lambda p=p: rows_of(p) for p in range(2)] + [
            lambda p=p: cols_of(p) for p in range(2)
        ]

    def each(step):
        return [lambda i=i: step(i) for i in range(0, edge, CHUNK)]

    return [
        each(enter),
        two_sided(left_a, right_a, arriving),
        each(second_slice),
        two_sided(left_f, right_f, field),
        each(residual),
        two_sided(left_f, right_f, field),
        each(second_grad),
        two_sided(left_a, right_a, field),
        each(first_grad),
    ]


def own_marks(part, base_row, edge, tile_rows):
    slots = part.shape[0] - 1
    first, second, left = [], [], []
    ranks = [jnp.int32(0), jnp.int32(0)]
    for q in range(slots):
        live = jnp.where(q < part[slots, 0], 1, 0)
        inner = jnp.where(part[q, 0] - base_row + edge <= tile_rows, live, 0)
        first.append(jnp.where(ranks[0] < EARLY, inner, 0))
        ranks[0] = ranks[0] + inner
        rest = live - first[q]
        second.append(jnp.where(ranks[1] < MIDDLE, rest, 0))
        ranks[1] = ranks[1] + rest
        left.append(rest - second[q])
    return first, second, left


def put_in_order(order, marks):
    taken = jnp.int32(0)
    order[0] = 0
    for q, mark in enumerate(marks):
        order[taken] = q
        taken = taken + mark
    return taken


def fill_corners(corner, part):
    for q in range(part.shape[0] - 1):
        corner[q, 0] = part[q, 0]
        corner[q, 1] = part[q, 1]


def list_late(order, corner, mine, across, base_row, edge, tile_rows):
    slots = mine.shape[0] - 1
    fill_corners(corner, mine)
    marks = own_marks(mine, base_row, edge, tile_rows)[2]
    for q in range(slots):
        corner[slots + q, 0] = across[q, 0]
        corner[slots + q, 1] = across[q, 1]
        marks.append(jnp.where(q < across[slots, 0], 1, 0))
    return put_in_order(order, marks)


def run_pairs(order, total, base_row, refs, work):
    def visit(step, carry):
        a = order[2 * step]
        b_lives = 2 * step + 1 < total
        b = jnp.where(b_lives, order[2 * step + 1], a)
        ones = slot_stages(a, 1.0, base_row, refs, work[0])
        twos = slot_stages(b, jnp.where(b_lives, 1.0, 0.0), base_row, refs, work[1])
        for step_now in ones[0]:
            step_now()
        for k in range(1, len(ones)):
            if k % 2:
                interleaved(ones[k], twos[k - 1])
            else:
                interleaved(twos[k - 1], ones[k])
        for step_now in twos[-1]:
            step_now()
        return carry

    lax.fori_loop(0, (total + 1) // 2, visit, 0)


def widen(wide, source, start, part, s_from, s_to):
    rows = source.shape[-2]
    for t in range(wide.shape[2]):
        wide[part, s_to, t, pl.ds(start, rows), :] = source[
            part, s_from, :, pl.ds(t * LANES, LANES)
        ].astype(jnp.float32)


def fetch(copies, sems):
    started = {}
    for k, (group, source, target) in enumerate(copies):
        copy = pltpu.make_async_copy(source, target, sems.at[k])
        copy.start()
        started.setdefault(group, []).append(copy)

    def wait(group):
        for copy in started[group]:
            copy.wait()

    return wait


def zero_rows(acc, start, rows):
    for part in range(2):
        for s in range(acc.shape[1]):
            for t in range(acc.shape[2]):
                acc[part, s, t, pl.ds(start, rows), :] = jnp.zeros((rows, LANES), jnp.float32)


def lay_patches(wide, wait, spec, rims, half):
    slices, tile_rows = spec.shape[1:3]
    wait("spec")
    for part in range(2):
        for s in range(slices):
            widen(wide, spec, 0, part, s, s)
    if rims:
        wait("rim")
        for part in range(2):
            widen(wide, rims[0], tile_rows, part, 0, half)
            widen(wide, rims[1], tile_rows, part, 0, 1 - half)


def early_kernel(
    meta,
    mine,
    probe_any,
    spec_any,
    amp_any,
    planes_any,
    acc,
    probe_acc,
    order,
    corner,
    sems,
    probe,
    spec,
    amp,
    planes,
    la,
    ra,
    lf,
    rf,
    wide,
    *work,
):
    wait = fetch(
        [
            ("spec", spec_any, spec),
            ("planes", planes_any, planes),
            ("rest", probe_any, probe),
            ("rest", amp_any, amp),
        ],
        sems,
    )
    tables = (la, ra, lf, rf)
    edge, tile_rows = probe.shape[1], spec.shape[2]
    zero_rows(acc, 0, tile_rows)
    probe_acc[...] = jnp.zeros(probe_acc.shape, jnp.float32)
    fill_corners(corner, mine)
    total = put_in_order(order, own_marks(mine, meta[0], edge, tile_rows)[0])
    lay_patches(wide, wait, spec, (), meta[1])
    wait("planes")
    lay_tables(planes, tables)
    wait("rest")
    refs = (corner, probe, amp, tables, wide, acc, probe_acc)
    run_pairs(order, total, meta[0], refs, (work[:5], work[5:]))


def middle_kernel(
    meta,
    mine,
    probe_any,
    spec_any,
    rim_own_any,
    rim_other_any,
    acc_any,
    probe_acc_any,
    amp_any,
    planes_any,
    acc,
    probe_acc,
    order,
    corner,
    sems,
    probe,
    spec,
    amp,
    planes,
    la,
    ra,
    lf,
    rf,
    wide,
    rim_own,
    rim_other,
    *work,
):
    edge, tile_rows = probe.shape[1], spec.shape[2]
    wait = fetch(
        [
            ("spec", spec_any, spec),
            ("planes", planes_any, planes),
            ("rim", rim_own_any, rim_own),
            ("rim", rim_other_any, rim_other),
            ("acc", acc_any, acc.at[:, :, :, pl.ds(0, tile_rows), :]),
            ("acc", probe_acc_any, probe_acc),
            ("rest", probe_any, probe),
            ("rest", amp_any, amp),
        ],
        sems,
    )
    tables = (la, ra, lf, rf)
    zero_rows(acc, tile_rows, edge)
    fill_corners(corner, mine)
    total = put_in_order(order, own_marks(mine, meta[0], edge, tile_rows)[1])
    lay_patches(wide, wait, spec, (rim_own, rim_other), meta[1])
    wait("planes")
    lay_tables(planes, tables)
    wait("acc")
    wait("rest")
    refs = (corner, probe, amp, tables, wide, acc, probe_acc)
    run_pairs(order, total, meta[0], refs, (work[:5], work[5:]))


def late_kernel(
    meta,
    mine,
    across,
    probe_any,
    spec_any,
    rim_own_any,
    rim_other_any,
    acc_any,
    probe_acc_any,
    amp_any,
    across_amp_any,
    planes_any,
    send_first,
    send_rows,
    keep_rim,
    keep_low,
    keep_top,
    keep_probe,
    order,
    corner,
    sems,
    probe,
    spec,
    amp,
    planes,
    la,
    ra,
    lf,
    rf,
    wide,
    rim_own,
    rim_other,
    acc,
    probe_acc,
    *work,
):
    tile_rows, width = spec.shape[2:]
    edge = probe.shape[1]
    slots = mine.shape[0] - 1
    wait = fetch(
        [
            ("spec", spec_any, spec),
            ("planes", planes_any, planes),
            ("rim", rim_own_any, rim_own),
            ("rim", rim_other_any, rim_other),
            ("acc", acc_any, acc),
            ("acc", probe_acc_any, probe_acc),
            ("rest", probe_any, probe),
            ("rest", amp_any, amp.at[pl.ds(0, slots)]),
            ("rest", across_amp_any, amp.at[pl.ds(slots, slots)]),
        ],
        sems,
    )
    tables = (la, ra, lf, rf)
    half = meta[1]
    other = 1 - half
    col_tiles = width // LANES
    total = list_late(order, corner, mine, across, meta[0], edge, tile_rows)
    lay_patches(wide, wait, spec, (rim_own, rim_other), half)
    wait("planes")
    lay_tables(planes, tables)
    wait("acc")
    wait("rest")
    refs = (corner, probe, amp, tables, wide, acc, probe_acc)
    run_pairs(order, total, meta[0], refs, (work[:5], work[5:]))

    below = pl.ds(tile_rows, edge)
    low = pl.ds(edge, tile_rows - edge)
    top = pl.ds(0, edge)
    rows = pl.ds(0, tile_rows)
    for part in range(2):
        sign = 1.0 if part == 0 else -1.0
        for t in range(col_tiles):
            cols = pl.ds(t * LANES, LANES)
            send_first[pl.ds(part * edge, edge), cols] = (
                sign * acc[part, other, t, below, :]
            ).astype(jnp.bfloat16)
            send_rows[part, :, cols] = (sign * acc[part, other, t, rows, :]).astype(jnp.bfloat16)
            keep_rim[part, :, cols] = sign * acc[part, half, t, below, :]
            keep_low[part, :, cols] = sign * acc[part, half, t, low, :]
            keep_top[part, :, cols] = sign * acc[part, half, t, top, :]
    deep = keep_probe.shape[0]
    flip = jnp.where(other == 1, -1.0, 1.0)
    for piece in range(width // edge):
        piece_rows, cols = pl.ds(piece * deep, deep), pl.ds(piece * edge, edge)
        send_first[pl.ds(2 * edge, deep), cols] = (flip * probe_acc[other, piece_rows, :]).astype(
            jnp.bfloat16
        )
        keep_probe[:, cols] = -flip * probe_acc[half, piece_rows, :]


VMEM = pl.BlockSpec(memory_space=pltpu.VMEM)
SMEM = pl.BlockSpec(memory_space=pltpu.SMEM)
ANY = pl.BlockSpec(memory_space=pl.ANY)


def scratch(entries, slices, width, tile_rows, rows, edge, copies):
    planes = pltpu.VMEM((2, edge, edge), jnp.float32)
    table = pltpu.VMEM((2 * edge, 2 * edge), jnp.bfloat16)
    stack = pltpu.VMEM((2 * edge, edge), jnp.bfloat16)
    joined = pltpu.VMEM((edge, 2 * edge), jnp.bfloat16)
    lead = [
        pltpu.SMEM((entries + 1,), jnp.int32),
        pltpu.SMEM((entries, 2), jnp.int32),
        pltpu.SemaphoreType.DMA((copies,)),
        planes,
        pltpu.VMEM((2, slices, tile_rows, width), jnp.bfloat16),
        pltpu.VMEM((entries, edge, edge), jnp.bfloat16),
        pltpu.VMEM((6, edge, edge), jnp.bfloat16),
        table,
        table,
        table,
        table,
        pltpu.VMEM((2, slices, width // LANES, rows, LANES), jnp.float32),
    ]
    return lead, [planes, planes, planes, stack, joined] * 2


def run_early(meta, mine, probe, spec, amp, planes):
    edge = probe.shape[1]
    _, slices, tile_rows, width = spec.shape
    lead, work = scratch(amp.shape[0], slices, width, tile_rows, tile_rows, edge, 4)
    return pl.pallas_call(
        early_kernel,
        out_shape=(
            jax.ShapeDtypeStruct((2, slices, width // LANES, tile_rows, LANES), jnp.float32),
            jax.ShapeDtypeStruct((2, edge, edge), jnp.float32),
        ),
        in_specs=[SMEM] * 2 + [ANY] * 4,
        out_specs=(VMEM, VMEM),
        scratch_shapes=lead + work,
        compiler_params=pltpu.CompilerParams(vmem_limit_bytes=24 * 1024 * 1024),
        name="early_slots",
    )(meta, mine, probe, spec, amp, planes)


def run_middle(meta, mine, probe, spec, rims, accs, amp, planes):
    edge = probe.shape[1]
    _, slices, tile_rows, width = spec.shape
    total = tile_rows + edge
    operands = (probe, spec, *rims, *accs, amp, planes)
    lead, work = scratch(amp.shape[0], slices, width, tile_rows, total, edge, len(operands))
    rim = pltpu.VMEM((2, 1, edge, width), jnp.bfloat16)
    return pl.pallas_call(
        middle_kernel,
        out_shape=(
            jax.ShapeDtypeStruct((2, slices, width // LANES, total, LANES), jnp.float32),
            jax.ShapeDtypeStruct((2, edge, edge), jnp.float32),
        ),
        in_specs=[SMEM] * 2 + [ANY] * len(operands),
        out_specs=(VMEM, VMEM),
        scratch_shapes=lead + [rim, rim] + work,
        compiler_params=pltpu.CompilerParams(vmem_limit_bytes=30 * 1024 * 1024),
        name="middle_slots",
    )(meta, mine, *operands)


def run_late(meta, lists, probe, spec, rims, accs, amps, planes):
    edge = probe.shape[1]
    _, slices, tile_rows, width = spec.shape
    total = tile_rows + edge
    deep = edge * edge // width
    operands = (probe, spec, *rims, *accs, *amps, planes)
    entries = sum(amp.shape[0] for amp in amps)
    lead, work = scratch(entries, slices, width, tile_rows, total, edge, len(operands))
    rim = pltpu.VMEM((2, 1, edge, width), jnp.bfloat16)
    return pl.pallas_call(
        late_kernel,
        out_shape=(
            jax.ShapeDtypeStruct((2 * edge + deep, width), jnp.bfloat16),
            jax.ShapeDtypeStruct((2, tile_rows, width), jnp.bfloat16),
            jax.ShapeDtypeStruct((2, edge, width), jnp.float32),
            jax.ShapeDtypeStruct((2, tile_rows - edge, width), jnp.float32),
            jax.ShapeDtypeStruct((2, edge, width), jnp.float32),
            jax.ShapeDtypeStruct((deep, width), jnp.float32),
        ),
        in_specs=[SMEM] * 3 + [ANY] * len(operands),
        out_specs=(VMEM,) * 6,
        scratch_shapes=lead
        + [
            rim,
            rim,
            pltpu.VMEM((2, slices, width // LANES, total, LANES), jnp.float32),
            pltpu.VMEM((2, edge, edge), jnp.float32),
        ]
        + work,
        compiler_params=pltpu.CompilerParams(vmem_limit_bytes=32 * 1024 * 1024),
        name="late_slots",
    )(meta, *lists, *operands)


def write_rows(meta, own, theirs, start, shape, base=None):
    slices, rows, width = shape[1], own.shape[1], own.shape[2]

    def kernel(meta, own, theirs, *rest):
        out, wide, sems = rest[-3:]
        half = meta[1]
        copies = []
        for s, source in ((half, own), (1 - half, theirs)):
            for part in range(2):
                wide[s, part] = source[part].astype(jnp.float32)
                copy = pltpu.make_async_copy(
                    wide.at[s, part],
                    out.at[part, s, pl.ds(start, rows), :],
                    sems.at[len(copies)],
                )
                copy.start()
                copies.append(copy)
        for copy in copies:
            copy.wait()

    extra = [] if base is None else [base]
    return pl.pallas_call(
        kernel,
        out_shape=jax.ShapeDtypeStruct(shape, jnp.float32),
        in_specs=[SMEM, VMEM, VMEM] + [ANY] * len(extra),
        out_specs=ANY,
        input_output_aliases={} if base is None else {3: 0},
        scratch_shapes=[
            pltpu.VMEM((slices, 2, rows, width), jnp.float32),
            pltpu.SemaphoreType.DMA((2 * slices,)),
        ],
        compiler_params=pltpu.CompilerParams(vmem_limit_bytes=16 * 1024 * 1024),
        cost_estimate=pl.CostEstimate(
            flops=0, bytes_accessed=2 * slices * rows * width * 6, transcendentals=0
        ),
        name="write_rows",
    )(meta, own, theirs, *extra)


def traded(value, axis, distance):
    count = lax.axis_size(axis)
    return lax.ppermute(value, axis, [(i, i ^ distance) for i in range(count)])


def passed_along(value, axis, steps):
    count = lax.axis_size(axis)
    initial, last = (max(0, -steps), min(count, count - steps))
    return lax.ppermute(value, axis, [(source, source + steps) for source in range(initial, last)])


def narrow_sum(own, got):
    return (own.astype(jnp.float32) + got.astype(jnp.float32)).astype(jnp.bfloat16)


def unfolded(value, edge):
    return jnp.concatenate([value[:, k : k + edge] for k in range(0, value.shape[1], edge)], 0)


def body(probe_field, specimen, amplitude, scan_anchor, counts):
    edge = probe_field.shape[1]
    _, slices, tile_rows, width = specimen.shape
    half = lax.axis_index("pos") % 2
    base_row = lax.axis_index("tile") * tile_rows
    meta = jnp.stack([base_row, half]).astype(jnp.int32)
    planes = fixed_tables(edge)
    rim_own = passed_along(
        lax.dynamic_slice(specimen, (0, half, 0, 0), (2, 1, edge, width)), "tile", -1
    )
    across_amp = traded(amplitude, "pos", 2)
    mine = jnp.concatenate([scan_anchor, jnp.broadcast_to(counts, (1, 2))], 0)
    across = traded(mine, "pos", 2)
    accs = run_early(meta, mine, probe_field, specimen, amplitude, planes)
    rim_own, accs = lax.optimization_barrier((rim_own, accs))
    rims = (rim_own, traded(rim_own, "pos", 1))
    accs = run_middle(meta, mine, probe_field, specimen, rims, accs, amplitude, planes)
    sent_first, sent_rows, kept_rim, kept_low, kept_top, kept_probe = run_late(
        meta,
        (mine, across),
        probe_field,
        specimen,
        rims,
        accs,
        (amplitude, across_amp),
        planes,
    )
    got_first = traded(sent_first, "pos", 1)
    got_first, sent_rows = lax.optimization_barrier((got_first, sent_rows))
    got_rows = traded(sent_rows, "pos", 1)
    below = kept_rim + got_first[: 2 * edge].reshape(kept_rim.shape).astype(jnp.float32)
    below = passed_along(below.astype(jnp.bfloat16), "tile", 1)
    probe_part = (kept_probe + got_first[2 * edge :].astype(jnp.float32)).astype(jnp.bfloat16)
    distance = lax.axis_size("tile")
    while distance > 1:
        distance //= 2
        probe_part = narrow_sum(probe_part, traded(probe_part, "tile", distance))
    lower = (kept_low + got_rows[:, edge:].astype(jnp.float32)).astype(jnp.bfloat16)
    tile_grad = write_rows(meta, lower, traded(lower, "pos", 1), edge, specimen.shape)
    top = kept_top + got_rows[:, :edge].astype(jnp.float32)
    below, top, tile_grad = lax.optimization_barrier((below, top, tile_grad))
    upper = (top + below.astype(jnp.float32)).astype(jnp.bfloat16)
    tile_grad = write_rows(meta, upper, traded(upper, "pos", 1), 0, specimen.shape, tile_grad)
    probe_theirs, tile_grad = lax.optimization_barrier((traded(probe_part, "pos", 1), tile_grad))
    probe_own, probe_theirs = [unfolded(value, edge) for value in (probe_part, probe_theirs)]
    probe_total = jnp.where(
        half == 0, jnp.stack([probe_own, probe_theirs]), jnp.stack([probe_theirs, probe_own])
    ).astype(jnp.float32)
    return (tile_grad, probe_total)


def solution(mesh):
    return jax.shard_map(
        body,
        mesh=mesh,
        in_specs=(
            P(),
            P(None, None, "tile", None),
            P(("tile", "pos"), None, None),
            P(("tile", "pos"), None),
            P(("tile", "pos")),
        ),
        out_specs=(P(None, None, "tile", None), P()),
        check_vma=False,
    )
```

profile of v0, /device:TPU:0, one launch (start us, length us, event | category | flops | bytes accessed | tf_op | source)
XLA Modules:
  0.0 80.8 jit_solution(5602683411328314132)
XLA Ops:
  0.6 0.0 copy-start.3
  0.7 1.2 %constant_dynamic-slice_fusion = bf16[2,1,256,512]{3,2,1,0:T(8,128)(2,1)S(1)} fusion(bf16[2,2,512,512]{3,2,1,0:T(8,128)(2,1)} %spec_any.5, s32[]{:T(128)S(6)} %select_n.19), kind=kLoop, calls=%fused_computation.14 | loop fusion | bytes 1048580 | tf_op jit(solution)/shard_map/dynamic_slice | solution.py:647
  1.8 1.3 %collective-permute-start.1 = (bf16[2,1,256,512]{3,2,1,0:T(8,128)(2,1)S(1)}, bf16[2,1,256,512]{3,2,1,0:T(8,128)(2,1)S(1)}, u32[]{:S(2)}, u32[]{:S(2)}) collective-permute-start(bf16[2,1,256,512]{3,2,1,0:T(8,128)(2,1)S(1)} %constant_dynamic-slice_fusion), channel_id=1, source_target_pairs={{4,0},{8,4},{12,8},{16,12},{20,16},{24,20},{28,24},{5,1},{9,5},{13... | collective-permute-start | bytes 1572872 | tf_op jit(solution)/shard_map/ppermute | solution.py:628
  3.1 3.0 %collective-permute-start.3 = (bf16[8,256,256]{2,1,0:T(8,128)(2,1)}, bf16[8,256,256]{2,1,0:T(8,128)(2,1)S(1)}, u32[]{:S(2)}, u32[]{:S(2)}) collective-permute-start(bf16[8,256,256]{2,1,0:T(8,128)(2,1)} %amp_any.5), channel_id=1, source_target_pairs={{0,2},{1,3},{2,0},{3,1},{4,6},{5,7},{6,4},{7,5},{8,10},{9,11},{10,... | collective-permute-start | bytes 3145736 | tf_op jit(solution)/shard_map/ppermute | solution.py:622
  6.8 0.8 copy.9
  7.6 0.1 pad_add_fusion.meta
  7.7 0.0 copy-start
  7.7 1.6 %copy-done = bf16[2,2,512,512]{3,2,1,0:T(8,128)(2,1)S(1)} copy-done((bf16[2,2,512,512]{3,2,1,0:T(8,128)(2,1)S(1)}, bf16[2,2,512,512]{3,2,1,0:T(8,128)(2,1)}, u32[]{:S(2)}) %copy-start) | copy-done | bytes 2097176
  9.2 1.2 %copy-done.2 = bf16[8,256,256]{2,1,0:T(8,128)(2,1)S(1)} copy-done((bf16[8,256,256]{2,1,0:T(8,128)(2,1)S(1)}, bf16[8,256,256]{2,1,0:T(8,128)(2,1)}, u32[]{:S(2)}) %copy-start.2) | copy-done | bytes 1048600
  10.5 1.1 %copy-done.4 = bf16[6,256,256]{2,1,0:T(8,128)(2,1)S(1)} copy-done((bf16[6,256,256]{2,1,0:T(8,128)(2,1)S(1)}, bf16[6,256,256]{2,1,0:T(8,128)(2,1)}, u32[]{:S(2)}) %copy-start.4) | copy-done | bytes 786456
  11.6 1.0 %copy-done.6 = f32[2,256,256]{2,1,0:T(8,128)S(1)} copy-done((f32[2,256,256]{2,1,0:T(8,128)S(1)}, f32[2,256,256]{2,1,0:T(8,128)}, u32[]{:S(2)}) %copy-start.6) | copy-done | bytes 524312
  12.6 9.3 %early_slots.1 = (f32[2,2,4,512,128]{4,3,2,1,0:T(8,128)S(1)}, f32[2,256,256]{2,1,0:T(8,128)S(1)}) custom-call(s32[2]{0:T(128)S(1)} %pad_add_fusion.meta, s32[9,2]{1,0:T(8,128)S(1)} %concatenate.9.mine, f32[2,256,256]{2,1,0:T(8,128)S(1)} %copy-done.6, bf16[2,2,512,512]{3,2,1,0:T(8,128)(2,1)S(1)} %copy-done, bf16[8,256,256]{2,1,0:T(8,128)(2,1)S(1)} %copy-done.2, ...), custom_call_target="tpu_custom_call" | custom-call | tf_op jit(solution)/shard_map/early_slots/pallas_call | solution.py:512
  21.9 0.0 collective-permute-done.1.rim_own_any
  22.0 0.1 collective-permute-start.2
  22.0 0.1 collective-permute-start
  22.1 1.8 %collective-permute-done.2.rim_other_any = bf16[2,1,256,512]{3,2,1,0:T(8,128)(2,1)S(1)} collective-permute-done((bf16[2,1,256,512]{3,2,1,0:T(8,128)(2,1)S(1)}, bf16[2,1,256,512]{3,2,1,0:T(8,128)(2,1)S(1)}, u32[]{:S(2)}, u32[]{:S(2)}) %collective-permute-start.2) | collective-permute-done | bytes 524320 | tf_op jit(solution)/shard_map/ppermute | solution.py:622
  23.9 0.0 copy-done.3
  23.9 0.0 copy-done.1
  23.9 0.0 copy-done.5
  23.9 0.0 copy-done.7
  24.0 2.1 %middle_slots.1 = (f32[2,2,4,768,128]{4,3,2,1,0:T(8,128)S(1)}, f32[2,256,256]{2,1,0:T(8,128)S(1)}) custom-call(s32[2]{0:T(128)S(1)} %pad_add_fusion.meta, s32[9,2]{1,0:T(8,128)S(1)} %concatenate.9.mine, f32[2,256,256]{2,1,0:T(8,128)S(1)} %copy-done.7, bf16[2,2,512,512]{3,2,1,0:T(8,128)(2,1)S(1)} %copy-done.1, ...), custom_call_target="tpu_custom_call" | custom-call | tf_op jit(solution)/shard_map/middle_slots/pallas_call | solution.py:533
  26.1 3.6 %collective-permute-done.across = s32[9,2]{1,0:T(8,128)S(1)} collective-permute-done((s32[9,2]{1,0:T(8,128)S(1)}, s32[9,2]{1,0:T(8,128)S(1)}, u32[]{:S(2)}, u32[]{:S(2)}) %collective-permute-start) | collective-permute-done | bytes 104 | tf_op jit(solution)/shard_map/ppermute | solution.py:622
  29.7 0.0 collective-permute-done.3.across_amp_any
  29.7 7.1 %late_slots.1 = (bf16[640,512]{1,0:T(8,128)(2,1)S(1)}, bf16[2,512,512]{2,1,0:T(8,128)(2,1)S(1)}, f32[2,256,512]{2,1,0:T(8,128)S(1)}, f32[2,256,512]{2,1,0:T(8,12...) custom-call(s32[2]{0:T(128)S(1)} %pad_add_fusion.meta, s32[9,2]{1,0:T(8,128)S(1)} %concatenate.9.mine, ...), custom_call_target="tpu_custom_call" | custom-call | tf_op jit(solution)/shard_map/late_slots/pallas_call | solution.py:556
  36.9 8.6 %collective-permute-start.4 = (bf16[640,512]{1,0:T(8,128)(2,1)S(1)}, bf16[640,512]{1,0:T(8,128)(2,1)S(1)}, u32[]{:S(2)}, u32[]{:S(2)}) collective-permute-start(bf16[640,512]{1,0:T(8,128)(2,1)S(1)} %get-tuple-element.30), channel_id=1, source_target_pairs={{0,1},{1,0},{2,3},{3,2},{4,5},{5,4},{6,7},{7,6},{8,9},{9,8},{10,11... | collective-permute-start | bytes 1966088 | tf_op jit(solution)/shard_map/ppermute | solution.py:622
  45.4 1.7 %collective-permute-done.4 = bf16[640,512]{1,0:T(8,128)(2,1)S(1)} collective-permute-done((bf16[640,512]{1,0:T(8,128)(2,1)S(1)}, bf16[640,512]{1,0:T(8,128)(2,1)S(1)}, u32[]{:S(2)}, u32[]{:S(2)}) %collective-permute-start.4) | collective-permute-done | bytes 655392 | tf_op jit(solution)/shard_map/ppermute | solution.py:622
  47.1 0.4 collective-permute-start.10
  47.6 0.6 collective-permute-start.5
  48.2 0.2 fusion
  48.4 9.8 %collective-permute-start.9 = (bf16[2,256,512]{2,1,0:T(8,128)(2,1)S(1)}, bf16[2,256,512]{2,1,0:T(8,128)(2,1)}, u32[]{:S(2)}, u32[]{:S(2)}) collective-permute-start(bf16[2,256,512]{2,1,0:T(8,128)(2,1)S(1)} %fusion), channel_id=1, source_target_pairs={{0,4},{4,8},{8,12},{12,16},{16,20},{20,24},{24,28},{1,5},{5,9},{9,... | collective-permute-start | bytes 1572872 | tf_op jit(solution)/shard_map/ppermute | solution.py:628
  58.2 0.0 collective-permute-done.10
  58.2 0.3 add_convert_fusion.1
  58.6 0.1 collective-permute-start.11
  58.6 0.0 collective-permute-done.5
  58.7 0.1 collective-permute-start.6
  58.8 5.9 %collective-permute-done.6 = bf16[128,512]{1,0:T(8,128)(2,1)S(1)} collective-permute-done((bf16[128,512]{1,0:T(8,128)(2,1)S(1)}, bf16[128,512]{1,0:T(8,128)(2,1)S(1)}, u32[]{:S(2)}, u32[]{:S(2)}) %collective-permute-start.6) | collective-permute-done | bytes 131104 | tf_op jit(solution)/shard_map/ppermute | solution.py:622
  64.7 8.2 %collective-permute-start.7 = (bf16[128,512]{1,0:T(8,128)(2,1)S(1)}, bf16[128,512]{1,0:T(8,128)(2,1)S(1)}, u32[]{:S(2)}, u32[]{:S(2)}) collective-permute-start(bf16[128,512]{1,0:T(8,128)(2,1)S(1)} %add_convert_fusion.3), channel_id=1, source_target_pairs={{0,4},{4,0},{8,12},{12,8},{16,20},{20,16},{24,28},{28,24},{1,5},{5... | collective-permute-start | bytes 393224 | tf_op jit(solution)/shard_map/ppermute | solution.py:622
  72.8 0.0 collective-permute-done.11.theirs
  72.8 1.9 %write_rows.2.rest_0_ = f32[2,2,512,512]{3,2,1,0:T(8,128)} custom-call(s32[2]{0:T(128)S(1)} %pad_add_fusion.meta, bf16[2,256,512]{2,1,0:T(8,128)(2,1)S(1)} %get-tuple-element.42.own, bf16[2,256,512]{2,1,0:T(8,128)(2,1)S(1)} %collective-permute-done.11.theirs), custom_call_target="tpu_custom_call" | custom-call | bytes 3145728 | tf_op jit(solution)/shard_map/write_rows/pallas_call | solution.py:602
  74.8 0.0 collective-permute-done.9
  74.8 1.2 %add_convert_fusion.own = bf16[2,256,512]{2,1,0:T(8,128)(2,1)S(1)} fusion(f32[2,256,512]{2,1,0:T(8,128)S(1)} %get-tuple-element.37, bf16[2,256,512]{2,1,0:T(8,128)(2,1)} %collective-permute-done.9), kind=kLoop, calls=%fused_computation.2 | loop fusion | flops 786432 | bytes 2097152 | tf_op jit(solution)/shard_map/convert_element_type | solution.py:680
  76.0 0.1 collective-permute-start.12
  76.1 0.1 collective-permute-done.7
  76.2 0.5 collective-permute-start.8
  76.7 1.3 %collective-permute-done.12.theirs = bf16[2,256,512]{2,1,0:T(8,128)(2,1)S(1)} collective-permute-done((bf16[2,256,512]{2,1,0:T(8,128)(2,1)S(1)}, bf16[2,256,512]{2,1,0:T(8,128)(2,1)S(1)}, u32[]{:S(2)}, u32[]{:S(2)}) %collective-permute-start.12) | collective-permute-done | bytes 524320 | tf_op jit(solution)/shard_map/ppermute | solution.py:622
  78.0 1.9 %write_rows.3 = f32[2,2,512,512]{3,2,1,0:T(8,128)} custom-call(s32[2]{0:T(128)S(1)} %pad_add_fusion.meta, bf16[2,256,512]{2,1,0:T(8,128)(2,1)S(1)} %add_convert_fusion.own, bf16[2,256,512]{2,1,0:T(8,128)(2,1)S(1)} %collective-permute-done.12.theirs, f32[2,2,512,512]{3,2,1,0:T(8,128)} %write_rows.2.rest_0_), custom_call_target="tpu_custom_call", output_to_operand_aliasing={{}: (3, {})} | custom-call | bytes 3145728 | tf_op jit(solution)/shard_map/write_rows/pallas_call | solution.py:602
  79.9 0.0 collective-permute-done.8
  79.9 0.8 %fusion.1 = f32[2,256,256]{2,1,0:T(8,128)} fusion(bf16[1,256,256]{2,1,0:T(8,128)(2,1)S(1)} %maximum_bitcast_fusion.1, bf16[1,256,256]{2,1,0:T(8,128)(2,1)S(1)} %maximum_bitcast_fusion, pred[]{:T(512)S(6)} %eq.5), kind=kLoop, calls=%fused_computation.6 | loop fusion | flops 524288 | bytes 786433 | tf_op jit(solution)/shard_map/convert_element_type | solution.py:686
  (16 shorter events, 0.2 us)
Async XLA Ops:
  0.6 23.3 %copy-start.3 = (bf16[8,256,256]{2,1,0:T(8,128)(2,1)S(1)}, bf16[8,256,256]{2,1,0:T(8,128)(2,1)}, u32[]{:S(2)}) copy-start(bf16[8,256,256]{2,1,0:T(8,128)(2,1)} %amp_any.5) | copy-start | bytes 3145732
  1.8 20.1 %collective-permute-start.1 = (bf16[2,1,256,512]{3,2,1,0:T(8,128)(2,1)S(1)}, bf16[2,1,256,512]{3,2,1,0:T(8,128)(2,1)S(1)}, u32[]{:S(2)}, u32[]{:S(2)}) collective-permute-start(bf16[2,1,256,512]{3,2,1,0:T(8,128)(2,1)S(1)} %constant_dynamic-slice_fusion), channel_id=1, source_target_pairs={{4,0},{8,4},{12,8},{16,12},{20,16},{24,20},{28,24},{5,1},{9,5},{13... | collective-permute-start | bytes 1572872 | tf_op jit(solution)/shard_map/ppermute | solution.py:628
  3.1 26.6 %collective-permute-start.3 = (bf16[8,256,256]{2,1,0:T(8,128)(2,1)}, bf16[8,256,256]{2,1,0:T(8,128)(2,1)S(1)}, u32[]{:S(2)}, u32[]{:S(2)}) collective-permute-start(bf16[8,256,256]{2,1,0:T(8,128)(2,1)} %amp_any.5), channel_id=1, source_target_pairs={{0,2},{1,3},{2,0},{3,1},{4,6},{5,7},{6,4},{7,5},{8,10},{9,11},{10,... | collective-permute-start | bytes 3145736 | tf_op jit(solution)/shard_map/ppermute | solution.py:622
  7.7 1.6 %copy-start = (bf16[2,2,512,512]{3,2,1,0:T(8,128)(2,1)S(1)}, bf16[2,2,512,512]{3,2,1,0:T(8,128)(2,1)}, u32[]{:S(2)}) copy-start(bf16[2,2,512,512]{3,2,1,0:T(8,128)(2,1)} %spec_any.5) | copy-start | bytes 6291460
  9.2 1.2 %copy-start.2 = (bf16[8,256,256]{2,1,0:T(8,128)(2,1)S(1)}, bf16[8,256,256]{2,1,0:T(8,128)(2,1)}, u32[]{:S(2)}) copy-start(bf16[8,256,256]{2,1,0:T(8,128)(2,1)} %amp_any.5) | copy-start | bytes 3145732
  10.5 1.1 %copy-start.4 = (bf16[6,256,256]{2,1,0:T(8,128)(2,1)S(1)}, bf16[6,256,256]{2,1,0:T(8,128)(2,1)}, u32[]{:S(2)}) copy-start(bf16[6,256,256]{2,1,0:T(8,128)(2,1)} %constant.27.clone.planes_any) | copy-start | bytes 2359300
  11.6 1.0 %copy-start.6 = (f32[2,256,256]{2,1,0:T(8,128)S(1)}, f32[2,256,256]{2,1,0:T(8,128)}, u32[]{:S(2)}) copy-start(f32[2,256,256]{2,1,0:T(8,128)} %probe_any.5) | copy-start | bytes 1572868
  12.6 11.3 %copy-start.1 = (bf16[2,2,512,512]{3,2,1,0:T(8,128)(2,1)S(1)}, bf16[2,2,512,512]{3,2,1,0:T(8,128)(2,1)}, u32[]{:S(2)}) copy-start(bf16[2,2,512,512]{3,2,1,0:T(8,128)(2,1)} %spec_any.5) | copy-start | bytes 6291460
  12.6 11.3 %copy-start.5 = (bf16[6,256,256]{2,1,0:T(8,128)(2,1)S(1)}, bf16[6,256,256]{2,1,0:T(8,128)(2,1)}, u32[]{:S(2)}) copy-start(bf16[6,256,256]{2,1,0:T(8,128)(2,1)} %constant.27.clone.planes_any) | copy-start | bytes 2359300
  12.6 11.3 %copy-start.7 = (f32[2,256,256]{2,1,0:T(8,128)S(1)}, f32[2,256,256]{2,1,0:T(8,128)}, u32[]{:S(2)}) copy-start(f32[2,256,256]{2,1,0:T(8,128)} %probe_any.5) | copy-start | bytes 1572868
  22.0 2.0 %collective-permute-start.2 = (bf16[2,1,256,512]{3,2,1,0:T(8,128)(2,1)S(1)}, bf16[2,1,256,512]{3,2,1,0:T(8,128)(2,1)S(1)}, u32[]{:S(2)}, u32[]{:S(2)}) collective-permute-start(bf16[2,1,256,512]{3,2,1,0:T(8,128)(2,1)S(1)} %collective-permute-done.1.rim_own_any), channel_id=1, source_target_pairs={{0,1},{1,0},{2,3},{3,2},{4,5},{5,4},{6,7},{7,6},{8,9},{9,8},{10,11... | collective-permute-start | bytes 1572872 | tf_op jit(solution)/shard_map/ppermute | solution.py:622
  22.0 7.7 %collective-permute-start = (s32[9,2]{1,0:T(8,128)S(1)}, s32[9,2]{1,0:T(8,128)S(1)}, u32[]{:S(2)}, u32[]{:S(2)}) collective-permute-start(s32[9,2]{1,0:T(8,128)S(1)} %concatenate.9.mine), channel_id=1, source_target_pairs={{0,2},{1,3},{2,0},{3,1},{4,6},{5,7},{6,4},{7,5},{8,10},{9,11},{10,... | collective-permute-start | bytes 224 | tf_op jit(solution)/shard_map/ppermute | solution.py:622
  36.9 10.3 %collective-permute-start.4 = (bf16[640,512]{1,0:T(8,128)(2,1)S(1)}, bf16[640,512]{1,0:T(8,128)(2,1)S(1)}, u32[]{:S(2)}, u32[]{:S(2)}) collective-permute-start(bf16[640,512]{1,0:T(8,128)(2,1)S(1)} %get-tuple-element.30), channel_id=1, source_target_pairs={{0,1},{1,0},{2,3},{3,2},{4,5},{5,4},{6,7},{7,6},{8,9},{9,8},{10,11... | collective-permute-start | bytes 1966088 | tf_op jit(solution)/shard_map/ppermute | solution.py:622
  47.1 11.1 %collective-permute-start.10 = (bf16[2,512,512]{2,1,0:T(8,128)(2,1)S(1)}, bf16[2,512,512]{2,1,0:T(8,128)(2,1)S(1)}, u32[]{:S(2)}, u32[]{:S(2)}) collective-permute-start(bf16[2,512,512]{2,1,0:T(8,128)(2,1)S(1)} %get-tuple-element.35), channel_id=1, source_target_pairs={{0,1},{1,0},{2,3},{3,2},{4,5},{5,4},{6,7},{7,6},{8,9},{9,8},{10,11... | collective-permute-start | bytes 3145736 | tf_op jit(solution)/shard_map/ppermute | solution.py:622
  47.6 11.0 %collective-permute-start.5 = (bf16[128,512]{1,0:T(8,128)(2,1)S(1)}, bf16[128,512]{1,0:T(8,128)(2,1)S(1)}, u32[]{:S(2)}, u32[]{:S(2)}) collective-permute-start(bf16[128,512]{1,0:T(8,128)(2,1)S(1)} %add_convert_fusion.5), channel_id=1, source_target_pairs={{0,16},{4,20},{8,24},{12,28},{16,0},{20,4},{24,8},{28,12},{1,17},{... | collective-permute-start | bytes 393224 | tf_op jit(solution)/shard_map/ppermute | solution.py:622
  48.4 26.4 %collective-permute-start.9 = (bf16[2,256,512]{2,1,0:T(8,128)(2,1)S(1)}, bf16[2,256,512]{2,1,0:T(8,128)(2,1)}, u32[]{:S(2)}, u32[]{:S(2)}) collective-permute-start(bf16[2,256,512]{2,1,0:T(8,128)(2,1)S(1)} %fusion), channel_id=1, source_target_pairs={{0,4},{4,8},{8,12},{12,16},{16,20},{20,24},{24,28},{1,5},{5,9},{9,... | collective-permute-start | bytes 1572872 | tf_op jit(solution)/shard_map/ppermute | solution.py:628
  58.6 14.3 %collective-permute-start.11 = (bf16[2,256,512]{2,1,0:T(8,128)(2,1)S(1)}, bf16[2,256,512]{2,1,0:T(8,128)(2,1)S(1)}, u32[]{:S(2)}, u32[]{:S(2)}) collective-permute-start(bf16[2,256,512]{2,1,0:T(8,128)(2,1)S(1)} %get-tuple-element.42.own), channel_id=1, source_target_pairs={{0,1},{1,0},{2,3},{3,2},{4,5},{5,4},{6,7},{7,6},{8,9},{9,8},{10,11... | collective-permute-start | bytes 1572872 | tf_op jit(solution)/shard_map/ppermute | solution.py:622
  58.7 6.0 %collective-permute-start.6 = (bf16[128,512]{1,0:T(8,128)(2,1)S(1)}, bf16[128,512]{1,0:T(8,128)(2,1)S(1)}, u32[]{:S(2)}, u32[]{:S(2)}) collective-permute-start(bf16[128,512]{1,0:T(8,128)(2,1)S(1)} %add_convert_fusion.4), channel_id=1, source_target_pairs={{0,8},{4,12},{8,0},{12,4},{16,24},{20,28},{24,16},{28,20},{1,9},{5... | collective-permute-start | bytes 393224 | tf_op jit(solution)/shard_map/ppermute | solution.py:622
  64.7 11.5 %collective-permute-start.7 = (bf16[128,512]{1,0:T(8,128)(2,1)S(1)}, bf16[128,512]{1,0:T(8,128)(2,1)S(1)}, u32[]{:S(2)}, u32[]{:S(2)}) collective-permute-start(bf16[128,512]{1,0:T(8,128)(2,1)S(1)} %add_convert_fusion.3), channel_id=1, source_target_pairs={{0,4},{4,0},{8,12},{12,8},{16,20},{20,16},{24,28},{28,24},{1,5},{5... | collective-permute-start | bytes 393224 | tf_op jit(solution)/shard_map/ppermute | solution.py:622
  76.0 2.0 %collective-permute-start.12 = (bf16[2,256,512]{2,1,0:T(8,128)(2,1)S(1)}, bf16[2,256,512]{2,1,0:T(8,128)(2,1)S(1)}, u32[]{:S(2)}, u32[]{:S(2)}) collective-permute-start(bf16[2,256,512]{2,1,0:T(8,128)(2,1)S(1)} %add_convert_fusion.own), channel_id=1, source_target_pairs={{0,1},{1,0},{2,3},{3,2},{4,5},{5,4},{6,7},{7,6},{8,9},{9,8},{10,11... | collective-permute-start | bytes 1572872 | tf_op jit(solution)/shard_map/ppermute | solution.py:622
  76.2 3.7 %collective-permute-start.8 = (bf16[128,512]{1,0:T(8,128)(2,1)S(1)}, bf16[128,512]{1,0:T(8,128)(2,1)S(1)}, u32[]{:S(2)}, u32[]{:S(2)}) collective-permute-start(bf16[128,512]{1,0:T(8,128)(2,1)S(1)} %add_convert_fusion.2), channel_id=1, source_target_pairs={{0,1},{1,0},{2,3},{3,2},{4,5},{5,4},{6,7},{7,6},{8,9},{9,8},{10,11... | collective-permute-start | bytes 393224 | tf_op jit(solution)/shard_map/ppermute | solution.py:622
where the time goes:
time: 80.7 us; the launch traced here: 80.8 us
  starting transfers between devices  32.7 us (41%)
  Pallas kernels  22.4 us (28%)
  waiting for transfers between devices  14.4 us (18%)
  local copies, waits for them, and re-layouts  6.99 us (9%)
  other arithmetic  2.78 us (3%)
  between operations  1.53 us (2%)
    ppermute x11, starting transfers between devices, traded(): return lax.ppermute(value, axis, [(i, i ^ distance) for i in range(count)])  21.6 us
    ppermute x11, waiting for transfers between devices, traded(): return lax.ppermute(value, axis, [(i, i ^ distance) for i in range(count)])  14.4 us
    ppermute x2, starting transfers between devices, passed_along(): lax.ppermute(value, axis, [(source, source + steps) for source in range(i...  11.1 us
    pallas_call x1, Pallas kernels, run_early(): pl.pallas_call(early_kernel, out_shape=(jax.ShapeDtypeStruct((2, slices,...  9.29 us
    pallas_call x1, Pallas kernels, run_late(): pl.pallas_call(late_kernel, out_shape=(jax.ShapeDtypeStruct((2 * edge + d...  7.15 us
    unnamed x17, local copies, waits for them, and re-layouts  5.76 us
    pallas_call x2, Pallas kernels, write_rows(): pl.pallas_call(kernel, out_shape=jax.ShapeDtypeStruct(shape, jnp.float32)...  3.84 us
    pallas_call x1, Pallas kernels, run_middle(): pl.pallas_call(middle_kernel, out_shape=(jax.ShapeDtypeStruct((2, slices,...  2.13 us
  transfers between devices with their start and end apart: 13, of which 6 were waited for; matrix products, arithmetic and copies ran while one was open for 3% of the time, Pallas kernels for 19%

commit v1 on v0

--- a/solution.py
+++ b/solution.py
@@ -617,6 +617,20 @@
     )(meta, own, theirs, *extra)
 
 
+def sum_rows(kept, got):
+    def kernel(kept, got, out):
+        out[...] = kept[...] + got[:, pl.ds(0, kept.shape[1]), :].astype(jnp.float32)
+
+    return pl.pallas_call(
+        kernel,
+        out_shape=jax.ShapeDtypeStruct(kept.shape, jnp.float32),
+        in_specs=[VMEM, VMEM],
+        out_specs=VMEM,
+        compiler_params=pltpu.CompilerParams(vmem_limit_bytes=8 * 1024 * 1024),
+        name="sum_rows",
+    )(kept, got)
+
+
 def traded(value, axis, distance):
     count = lax.axis_size(axis)
     return lax.ppermute(value, axis, [(i, i ^ distance) for i in range(count)])
@@ -669,16 +683,23 @@
     below = kept_rim + got_first[: 2 * edge].reshape(kept_rim.shape).astype(jnp.float32)
     below = passed_along(below.astype(jnp.bfloat16), "tile", 1)
     probe_part = (kept_probe + got_first[2 * edge :].astype(jnp.float32)).astype(jnp.bfloat16)
+    got_probe = jnp.zeros_like(probe_part)
     distance = lax.axis_size("tile")
-    while distance > 1:
+    while distance > 4:
         distance //= 2
-        probe_part = narrow_sum(probe_part, traded(probe_part, "tile", distance))
+        probe_part = narrow_sum(probe_part, got_probe)
+        got_probe = traded(probe_part, "tile", distance)
     lower = (kept_low + got_rows[:, edge:].astype(jnp.float32)).astype(jnp.bfloat16)
     tile_grad = write_rows(meta, lower, traded(lower, "pos", 1), edge, specimen.shape)
-    top = kept_top + got_rows[:, :edge].astype(jnp.float32)
-    below, top, tile_grad = lax.optimization_barrier((below, top, tile_grad))
+    top = sum_rows(kept_top, got_rows)
+    got_probe, top, tile_grad = lax.optimization_barrier((got_probe, top, tile_grad))
+    probe_part = narrow_sum(probe_part, got_probe)
+    below, top, probe_part = lax.optimization_barrier((below, top, probe_part))
     upper = (top + below.astype(jnp.float32)).astype(jnp.bfloat16)
-    tile_grad = write_rows(meta, upper, traded(upper, "pos", 1), 0, specimen.shape, tile_grad)
+    upper_theirs = traded(upper, "pos", 1)
+    near = [traded(probe_part, "tile", d).astype(jnp.float32) for d in range(1, distance)]
+    probe_part = (probe_part.astype(jnp.float32) + sum(near)).astype(jnp.bfloat16)
+    tile_grad = write_rows(meta, upper, upper_theirs, 0, specimen.shape, tile_grad)
     probe_theirs, tile_grad = lax.optimization_barrier((traded(probe_part, "pos", 1), tile_grad))
     probe_own, probe_theirs = [unfolded(value, edge) for value in (probe_part, probe_theirs)]
     probe_total = jnp.where(

time: 80.7 us -> 91.1 us (1.13); the launches traced: 80.8 us -> 89.4 us
  starting transfers between devices: 32.7 us -> 20.3 us
  waiting for transfers between devices: 14.4 us -> 24.6 us
  Pallas kernels: 22.4 us -> 30.3 us
  local copies, waits for them, and re-layouts: 6.99 us -> 9.19 us
    pallas_call x1, Pallas kernels: 7.15 us -> 18.7 us  [run_late(): pl.pallas_call(late_kernel, out_shape=(jax.ShapeDtypeStruct((2 * edge + d...]
    ppermute x2, starting transfers between devices: 11.1 us -> 3.39 us  [passed_along(): lax.ppermute(value, axis, [(source, source + steps) for source in range(i...]
    ppermute x11 -> x12, waiting for transfers between devices: 14.4 us -> 19.5 us  [traded(): return lax.ppermute(value, axis, [(i, i ^ distance) for i in range(count)])]
    ppermute x2, waiting for transfers between devices: 0.01 us -> 5.08 us  [passed_along(): lax.ppermute(value, axis, [(source, source + steps) for source in range(i...]
    ppermute x11 -> x12, starting transfers between devices: 21.6 us -> 16.9 us  [traded(): return lax.ppermute(value, axis, [(i, i ^ distance) for i in range(count)])]
    pallas_call x1, Pallas kernels: 9.29 us -> 5.53 us  [run_early(): pl.pallas_call(early_kernel, out_shape=(jax.ShapeDtypeStruct((2, slices,...]
    unnamed x17 -> x21, local copies, waits for them, and re-layouts: 5.76 us -> 7.96 us
  transfers between devices with their start and end apart: 13 -> 14, of which waited for: 6 -> 8; matrix products, arithmetic and copies ran while one was open for 3% -> 4% of each run, Pallas kernels for 19% -> 13%
where the time goes in v1:
time: 91.1 us; the launch traced here: 89.4 us
  Pallas kernels  30.3 us (33%)
  waiting for transfers between devices  24.6 us (27%)
  starting transfers between devices  20.3 us (22%)
  local copies, waits for them, and re-layouts  9.19 us (10%)
  other arithmetic  3.46 us (4%)
  between operations  1.5 us (2%)
    ppermute x12, waiting for transfers between devices, traded(): return lax.ppermute(value, axis, [(i, i ^ distance) for i in range(count)])  19.5 us
    pallas_call x1, Pallas kernels, run_late(): pl.pallas_call(late_kernel, out_shape=(jax.ShapeDtypeStruct((2 * edge + d...  18.7 us
    ppermute x12, starting transfers between devices, traded(): return lax.ppermute(value, axis, [(i, i ^ distance) for i in range(count)])  16.9 us
    unnamed x21, local copies, waits for them, and re-layouts  7.96 us
    pallas_call x1, Pallas kernels, run_early(): pl.pallas_call(early_kernel, out_shape=(jax.ShapeDtypeStruct((2, slices,...  5.53 us
    ppermute x2, waiting for transfers between devices, passed_along(): lax.ppermute(value, axis, [(source, source + steps) for source in range(i...  5.08 us
    pallas_call x2, Pallas kernels, write_rows(): pl.pallas_call(kernel, out_shape=jax.ShapeDtypeStruct(shape, jnp.float32)...  3.85 us
    ppermute x2, starting transfers between devices, passed_along(): lax.ppermute(value, axis, [(source, source + steps) for source in range(i...  3.39 us
  transfers between devices with their start and end apart: 14, of which 8 were waited for; matrix products, arithmetic and copies ran while one was open for 4% of the time, Pallas kernels for 13%

profile of v1, /device:TPU:0, one launch (start us, length us, event | category | flops | bytes accessed | tf_op | source)
XLA Modules:
  0.0 89.4 jit_solution(5942380264225669013)
XLA Ops:
  0.6 0.0 copy-start.3
  0.7 1.2 %constant_dynamic-slice_fusion = bf16[2,1,256,512]{3,2,1,0:T(8,128)(2,1)S(1)} fusion(bf16[2,2,512,512]{3,2,1,0:T(8,128)(2,1)} %spec_any.5, s32[]{:T(128)S(6)} %select_n.19), kind=kLoop, calls=%fused_computation.12 | loop fusion | bytes 1048580 | tf_op jit(solution)/shard_map/dynamic_slice | solution.py:661
  1.8 1.3 %collective-permute-start.1 = (bf16[2,1,256,512]{3,2,1,0:T(8,128)(2,1)S(1)}, bf16[2,1,256,512]{3,2,1,0:T(8,128)(2,1)S(1)}, u32[]{:S(2)}, u32[]{:S(2)}) collective-permute-start(bf16[2,1,256,512]{3,2,1,0:T(8,128)(2,1)S(1)} %constant_dynamic-slice_fusion), channel_id=1, source_target_pairs={{4,0},{8,4},{12,8},{16,12},{20,16},{24,20},{28,24},{5,1},{9,5},{13... | collective-permute-start | bytes 1572872 | tf_op jit(solution)/shard_map/ppermute | solution.py:642
  3.1 3.0 %collective-permute-start.3 = (bf16[8,256,256]{2,1,0:T(8,128)(2,1)}, bf16[8,256,256]{2,1,0:T(8,128)(2,1)S(1)}, u32[]{:S(2)}, u32[]{:S(2)}) collective-permute-start(bf16[8,256,256]{2,1,0:T(8,128)(2,1)} %amp_any.5), channel_id=1, source_target_pairs={{0,2},{1,3},{2,0},{3,1},{4,6},{5,7},{6,4},{7,5},{8,10},{9,11},{10,... | collective-permute-start | bytes 3145736 | tf_op jit(solution)/shard_map/ppermute | solution.py:636
  6.8 0.8 copy.9
  7.6 0.1 pad_add_fusion.meta
  7.7 1.6 %copy-done = bf16[2,2,512,512]{3,2,1,0:T(8,128)(2,1)S(1)} copy-done((bf16[2,2,512,512]{3,2,1,0:T(8,128)(2,1)S(1)}, bf16[2,2,512,512]{3,2,1,0:T(8,128)(2,1)}, u32[]{:S(2)}) %copy-start) | copy-done | bytes 2097176
  9.2 1.2 %copy-done.2 = bf16[8,256,256]{2,1,0:T(8,128)(2,1)S(1)} copy-done((bf16[8,256,256]{2,1,0:T(8,128)(2,1)S(1)}, bf16[8,256,256]{2,1,0:T(8,128)(2,1)}, u32[]{:S(2)}) %copy-start.2) | copy-done | bytes 1048600
  10.5 1.1 %copy-done.4 = bf16[6,256,256]{2,1,0:T(8,128)(2,1)S(1)} copy-done((bf16[6,256,256]{2,1,0:T(8,128)(2,1)S(1)}, bf16[6,256,256]{2,1,0:T(8,128)(2,1)}, u32[]{:S(2)}) %copy-start.4) | copy-done | bytes 786456
  11.6 1.0 %copy-done.6 = f32[2,256,256]{2,1,0:T(8,128)S(1)} copy-done((f32[2,256,256]{2,1,0:T(8,128)S(1)}, f32[2,256,256]{2,1,0:T(8,128)}, u32[]{:S(2)}) %copy-start.6) | copy-done | bytes 524312
  12.6 5.5 %early_slots.1 = (f32[2,2,4,512,128]{4,3,2,1,0:T(8,128)S(1)}, f32[2,256,256]{2,1,0:T(8,128)S(1)}) custom-call(s32[2]{0:T(128)S(1)} %pad_add_fusion.meta, s32[9,2]{1,0:T(8,128)S(1)} %concatenate.9.mine, f32[2,256,256]{2,1,0:T(8,128)S(1)} %copy-done.6, bf16[2,2,512,512]{3,2,1,0:T(8,128)(2,1)S(1)} %copy-done, bf16[8,256,256]{2,1,0:T(8,128)(2,1)S(1)} %copy-done.2, ...), custom_call_target="tpu_custom_call" | custom-call | tf_op jit(solution)/shard_map/early_slots/pallas_call | solution.py:512
  18.2 0.4 collective-permute-done.1.rim_own_any
  18.6 0.0 collective-permute-start.2
  18.6 1.8 %collective-permute-start = (s32[9,2]{1,0:T(8,128)S(1)}, s32[9,2]{1,0:T(8,128)S(1)}, u32[]{:S(2)}, u32[]{:S(2)}) collective-permute-start(s32[9,2]{1,0:T(8,128)S(1)} %concatenate.9.mine), channel_id=1, source_target_pairs={{0,2},{1,3},{2,0},{3,1},{4,6},{5,7},{6,4},{7,5},{8,10},{9,11},{10,... | collective-permute-start | bytes 224 | tf_op jit(solution)/shard_map/ppermute | solution.py:636
  20.4 0.1 collective-permute-done.2.rim_other_any
  20.5 2.1 %middle_slots.1 = (f32[2,2,4,768,128]{4,3,2,1,0:T(8,128)S(1)}, f32[2,256,256]{2,1,0:T(8,128)S(1)}) custom-call(s32[2]{0:T(128)S(1)} %pad_add_fusion.meta, s32[9,2]{1,0:T(8,128)S(1)} %concatenate.9.mine, f32[2,256,256]{2,1,0:T(8,128)S(1)} %copy-done.7, bf16[2,2,512,512]{3,2,1,0:T(8,128)(2,1)S(1)} %copy-done.1, ...), custom_call_target="tpu_custom_call" | custom-call | tf_op jit(solution)/shard_map/middle_slots/pallas_call | solution.py:533
  22.7 7.1 %collective-permute-done.across = s32[9,2]{1,0:T(8,128)S(1)} collective-permute-done((s32[9,2]{1,0:T(8,128)S(1)}, s32[9,2]{1,0:T(8,128)S(1)}, u32[]{:S(2)}, u32[]{:S(2)}) %collective-permute-start) | collective-permute-done | bytes 104 | tf_op jit(solution)/shard_map/ppermute | solution.py:636
  29.7 0.0 collective-permute-done.3.across_amp_any
  29.7 1.0 %copy-done.8 = bf16[8,256,256]{2,1,0:T(8,128)(2,1)} copy-done((bf16[8,256,256]{2,1,0:T(8,128)(2,1)}, bf16[8,256,256]{2,1,0:T(8,128)(2,1)S(1)}, u32[]{:S(2)}) %copy-start.8) | copy-done | bytes 1048600
  30.7 1.2 %copy-done.9 = bf16[8,256,256]{2,1,0:T(8,128)(2,1)S(1)} copy-done((bf16[8,256,256]{2,1,0:T(8,128)(2,1)S(1)}, bf16[8,256,256]{2,1,0:T(8,128)(2,1)}, u32[]{:S(2)}) %copy-start.9) | copy-done | bytes 1048600
  31.9 18.7 %late_slots.1 = (bf16[640,512]{1,0:T(8,128)(2,1)S(1)}, bf16[2,512,512]{2,1,0:T(8,128)(2,1)S(1)}, f32[2,256,512]{2,1,0:T(8,128)S(1)}, f32[2,256,512]{2,1,0:T(8,12...) custom-call(s32[2]{0:T(128)S(1)} %pad_add_fusion.meta, s32[9,2]{1,0:T(8,128)S(1)} %concatenate.9.mine, ...), custom_call_target="tpu_custom_call" | custom-call | tf_op jit(solution)/shard_map/late_slots/pallas_call | solution.py:556
  50.7 0.1 collective-permute-start.4
  50.7 2.1 %collective-permute-done.4 = bf16[640,512]{1,0:T(8,128)(2,1)S(1)} collective-permute-done((bf16[640,512]{1,0:T(8,128)(2,1)S(1)}, bf16[640,512]{1,0:T(8,128)(2,1)S(1)}, u32[]{:S(2)}, u32[]{:S(2)}) %collective-permute-start.4) | collective-permute-done | bytes 655392 | tf_op jit(solution)/shard_map/ppermute | solution.py:636
  52.8 0.1 collective-permute-start.7
  53.0 2.5 %collective-permute-done.7.got = bf16[2,512,512]{2,1,0:T(8,128)(2,1)S(1)} collective-permute-done((bf16[2,512,512]{2,1,0:T(8,128)(2,1)S(1)}, bf16[2,512,512]{2,1,0:T(8,128)(2,1)S(1)}, u32[]{:S(2)}, u32[]{:S(2)}) %collective-permute-start.7) | collective-permute-done | bytes 1048608 | tf_op jit(solution)/shard_map/ppermute | solution.py:636
  55.5 0.2 add_convert_fusion.1.own
  55.7 0.2 collective-permute-start.8
  55.9 1.0 %fusion = bf16[2,256,512]{2,1,0:T(8,128)(2,1)} fusion(f32[2,256,512]{2,1,0:T(8,128)S(1)} %get-tuple-element.32, bf16[2,256,512]{2,1,0:T(8,128)(2,1)S(1)} %bitcast.10), kind=kLoop, calls=%fused_computation.1 | loop fusion | flops 786432 | bytes 2097152 | tf_op jit(solution)/shard_map/convert_element_type | solution.py:684
  56.8 2.1 %collective-permute-start.5 = (bf16[2,256,512]{2,1,0:T(8,128)(2,1)}, bf16[2,256,512]{2,1,0:T(8,128)(2,1)}, u32[]{:S(2)}, u32[]{:S(2)}) collective-permute-start(bf16[2,256,512]{2,1,0:T(8,128)(2,1)} %fusion), channel_id=1, source_target_pairs={{0,4},{4,8},{8,12},{12,16},{16,20},{20,24},{24,28},{1,5},{5,9},{9,... | collective-permute-start | bytes 1572872 | tf_op jit(solution)/shard_map/ppermute | solution.py:642
  59.0 1.4 %collective-permute-start.6 = (bf16[128,512]{1,0:T(8,128)(2,1)S(1)}, bf16[128,512]{1,0:T(8,128)(2,1)S(1)}, u32[]{:S(2)}, u32[]{:S(2)}) collective-permute-start(bf16[128,512]{1,0:T(8,128)(2,1)S(1)} %add_convert_fusion.4), channel_id=1, source_target_pairs={{0,16},{4,20},{8,24},{12,28},{16,0},{20,4},{24,8},{28,12},{1,17},{... | collective-permute-start | bytes 393224 | tf_op jit(solution)/shard_map/ppermute | solution.py:636
  60.3 0.1 sum_rows.1
  60.4 0.0 collective-permute-done.8.theirs
  60.4 1.9 %write_rows.2.rest_0_ = f32[2,2,512,512]{3,2,1,0:T(8,128)} custom-call(s32[2]{0:T(128)S(1)} %pad_add_fusion.meta, bf16[2,256,512]{2,1,0:T(8,128)(2,1)S(1)} %add_convert_fusion.1.own, bf16[2,256,512]{2,1,0:T(8,128)(2,1)S(1)} %collective-permute-done.8.theirs), custom_call_target="tpu_custom_call" | custom-call | bytes 3145728 | tf_op jit(solution)/shard_map/write_rows/pallas_call | solution.py:602
  62.4 3.3 %collective-permute-done.6 = bf16[128,512]{1,0:T(8,128)(2,1)S(1)} collective-permute-done((bf16[128,512]{1,0:T(8,128)(2,1)S(1)}, bf16[128,512]{1,0:T(8,128)(2,1)S(1)}, u32[]{:S(2)}, u32[]{:S(2)}) %collective-permute-start.6) | collective-permute-done | bytes 131104 | tf_op jit(solution)/shard_map/ppermute | solution.py:636
  65.8 4.7 %collective-permute-done.5 = bf16[2,256,512]{2,1,0:T(8,128)(2,1)} collective-permute-done((bf16[2,256,512]{2,1,0:T(8,128)(2,1)}, bf16[2,256,512]{2,1,0:T(8,128)(2,1)}, u32[]{:S(2)}, u32[]{:S(2)}) %collective-permute-start.5) | collective-permute-done | bytes 524320 | tf_op jit(solution)/shard_map/ppermute | solution.py:642
  70.4 6.7 %collective-permute-start.11 = (bf16[128,512]{1,0:T(8,128)(2,1)S(1)}, bf16[128,512]{1,0:T(8,128)(2,1)S(1)}, u32[]{:S(2)}, u32[]{:S(2)}) collective-permute-start(bf16[128,512]{1,0:T(8,128)(2,1)S(1)} %add_convert_fusion.3), channel_id=1, source_target_pairs={{0,12},{4,8},{8,4},{12,0},{16,28},{20,24},{24,20},{28,16},{1,13},{... | collective-permute-start | bytes 393224 | tf_op jit(solution)/shard_map/ppermute | solution.py:636
  77.1 3.5 %collective-permute-start.10 = (bf16[128,512]{1,0:T(8,128)(2,1)S(1)}, bf16[128,512]{1,0:T(8,128)(2,1)S(1)}, u32[]{:S(2)}, u32[]{:S(2)}) collective-permute-start(bf16[128,512]{1,0:T(8,128)(2,1)S(1)} %add_convert_fusion.3), channel_id=1, source_target_pairs={{0,8},{4,12},{8,0},{12,4},{16,24},{20,28},{24,16},{28,20},{1,9},{5... | collective-permute-start | bytes 393224 | tf_op jit(solution)/shard_map/ppermute | solution.py:636
  80.6 0.0 collective-permute-start.9
  80.6 1.2 %add_convert_fusion.own = bf16[2,256,512]{2,1,0:T(8,128)(2,1)S(1)} fusion(f32[2,256,512]{2,1,0:T(8,128)S(1)} %sum_rows.1, bf16[2,256,512]{2,1,0:T(8,128)(2,1)} %collective-permute-done.5), kind=kLoop, calls=%fused_computation.2 | loop fusion | flops 786432 | bytes 2097152 | tf_op jit(solution)/shard_map/convert_element_type | solution.py:698
  81.9 0.1 collective-permute-start.13
  82.0 0.0 collective-permute-done.11
  82.0 4.4 %collective-permute-done.10 = bf16[128,512]{1,0:T(8,128)(2,1)S(1)} collective-permute-done((bf16[128,512]{1,0:T(8,128)(2,1)S(1)}, bf16[128,512]{1,0:T(8,128)(2,1)S(1)}, u32[]{:S(2)}, u32[]{:S(2)}) %collective-permute-start.10) | collective-permute-done | bytes 131104 | tf_op jit(solution)/shard_map/ppermute | solution.py:636
  86.4 0.0 collective-permute-done.9
  86.4 0.1 add_convert_fusion.2
  86.5 0.1 collective-permute-start.12
  86.6 1.9 %write_rows.3 = f32[2,2,512,512]{3,2,1,0:T(8,128)} custom-call(s32[2]{0:T(128)S(1)} %pad_add_fusion.meta, bf16[2,256,512]{2,1,0:T(8,128)(2,1)S(1)} %add_convert_fusion.own, bf16[2,256,512]{2,1,0:T(8,128)(2,1)S(1)} %collective-permute-done.13.theirs, f32[2,2,512,512]{3,2,1,0:T(8,128)} %write_rows.2.rest_0_), custom_call_target="tpu_custom_call", output_to_operand_aliasing={{}: (3, {})} | custom-call | bytes 3145728 | tf_op jit(solution)/shard_map/write_rows/pallas_call | solution.py:602
  88.5 0.0 collective-permute-done.12
  88.6 0.8 fusion.1
  (22 shorter events, 0.2 us)
Async XLA Ops:
  0.6 19.9 %copy-start.3 = (bf16[8,256,256]{2,1,0:T(8,128)(2,1)S(1)}, bf16[8,256,256]{2,1,0:T(8,128)(2,1)}, u32[]{:S(2)}) copy-start(bf16[8,256,256]{2,1,0:T(8,128)(2,1)} %amp_any.5) | copy-start | bytes 3145732
  1.8 16.8 %collective-permute-start.1 = (bf16[2,1,256,512]{3,2,1,0:T(8,128)(2,1)S(1)}, bf16[2,1,256,512]{3,2,1,0:T(8,128)(2,1)S(1)}, u32[]{:S(2)}, u32[]{:S(2)}) collective-permute-start(bf16[2,1,256,512]{3,2,1,0:T(8,128)(2,1)S(1)} %constant_dynamic-slice_fusion), channel_id=1, source_target_pairs={{4,0},{8,4},{12,8},{16,12},{20,16},{24,20},{28,24},{5,1},{9,5},{13... | collective-permute-start | bytes 1572872 | tf_op jit(solution)/shard_map/ppermute | solution.py:642
  3.1 26.6 %collective-permute-start.3 = (bf16[8,256,256]{2,1,0:T(8,128)(2,1)}, bf16[8,256,256]{2,1,0:T(8,128)(2,1)S(1)}, u32[]{:S(2)}, u32[]{:S(2)}) collective-permute-start(bf16[8,256,256]{2,1,0:T(8,128)(2,1)} %amp_any.5), channel_id=1, source_target_pairs={{0,2},{1,3},{2,0},{3,1},{4,6},{5,7},{6,4},{7,5},{8,10},{9,11},{10,... | collective-permute-start | bytes 3145736 | tf_op jit(solution)/shard_map/ppermute | solution.py:636
  7.7 1.6 %copy-start = (bf16[2,2,512,512]{3,2,1,0:T(8,128)(2,1)S(1)}, bf16[2,2,512,512]{3,2,1,0:T(8,128)(2,1)}, u32[]{:S(2)}) copy-start(bf16[2,2,512,512]{3,2,1,0:T(8,128)(2,1)} %spec_any.5) | copy-start | bytes 6291460
  9.2 1.2 %copy-start.2 = (bf16[8,256,256]{2,1,0:T(8,128)(2,1)S(1)}, bf16[8,256,256]{2,1,0:T(8,128)(2,1)}, u32[]{:S(2)}) copy-start(bf16[8,256,256]{2,1,0:T(8,128)(2,1)} %amp_any.5) | copy-start | bytes 3145732
  10.5 1.1 %copy-start.4 = (bf16[6,256,256]{2,1,0:T(8,128)(2,1)S(1)}, bf16[6,256,256]{2,1,0:T(8,128)(2,1)}, u32[]{:S(2)}) copy-start(bf16[6,256,256]{2,1,0:T(8,128)(2,1)} %constant.27.clone.planes_any) | copy-start | bytes 2359300
  11.6 1.0 %copy-start.6 = (f32[2,256,256]{2,1,0:T(8,128)S(1)}, f32[2,256,256]{2,1,0:T(8,128)}, u32[]{:S(2)}) copy-start(f32[2,256,256]{2,1,0:T(8,128)} %probe_any.5) | copy-start | bytes 1572868
  12.6 7.9 %copy-start.1 = (bf16[2,2,512,512]{3,2,1,0:T(8,128)(2,1)S(1)}, bf16[2,2,512,512]{3,2,1,0:T(8,128)(2,1)}, u32[]{:S(2)}) copy-start(bf16[2,2,512,512]{3,2,1,0:T(8,128)(2,1)} %spec_any.5) | copy-start | bytes 6291460
  12.6 7.9 %copy-start.5 = (bf16[6,256,256]{2,1,0:T(8,128)(2,1)S(1)}, bf16[6,256,256]{2,1,0:T(8,128)(2,1)}, u32[]{:S(2)}) copy-start(bf16[6,256,256]{2,1,0:T(8,128)(2,1)} %constant.27.clone.planes_any) | copy-start | bytes 2359300
  12.6 7.9 %copy-start.7 = (f32[2,256,256]{2,1,0:T(8,128)S(1)}, f32[2,256,256]{2,1,0:T(8,128)}, u32[]{:S(2)}) copy-start(f32[2,256,256]{2,1,0:T(8,128)} %probe_any.5) | copy-start | bytes 1572868
  18.6 1.9 %collective-permute-start.2 = (bf16[2,1,256,512]{3,2,1,0:T(8,128)(2,1)S(1)}, bf16[2,1,256,512]{3,2,1,0:T(8,128)(2,1)S(1)}, u32[]{:S(2)}, u32[]{:S(2)}) collective-permute-start(bf16[2,1,256,512]{3,2,1,0:T(8,128)(2,1)S(1)} %collective-permute-done.1.rim_own_any), channel_id=1, source_target_pairs={{0,1},{1,0},{2,3},{3,2},{4,5},{5,4},{6,7},{7,6},{8,9},{9,8},{10,11... | collective-permute-start | bytes 1572872 | tf_op jit(solution)/shard_map/ppermute | solution.py:636
  18.6 11.1 %collective-permute-start = (s32[9,2]{1,0:T(8,128)S(1)}, s32[9,2]{1,0:T(8,128)S(1)}, u32[]{:S(2)}, u32[]{:S(2)}) collective-permute-start(s32[9,2]{1,0:T(8,128)S(1)} %concatenate.9.mine), channel_id=1, source_target_pairs={{0,2},{1,3},{2,0},{3,1},{4,6},{5,7},{6,4},{7,5},{8,10},{9,11},{10,... | collective-permute-start | bytes 224 | tf_op jit(solution)/shard_map/ppermute | solution.py:636
  29.7 1.0 %copy-start.8 = (bf16[8,256,256]{2,1,0:T(8,128)(2,1)}, bf16[8,256,256]{2,1,0:T(8,128)(2,1)S(1)}, u32[]{:S(2)}) copy-start(bf16[8,256,256]{2,1,0:T(8,128)(2,1)S(1)} %collective-permute-done.3.across_amp_any) | copy-start | bytes 3145732
  30.7 1.2 %copy-start.9 = (bf16[8,256,256]{2,1,0:T(8,128)(2,1)S(1)}, bf16[8,256,256]{2,1,0:T(8,128)(2,1)}, u32[]{:S(2)}) copy-start(bf16[8,256,256]{2,1,0:T(8,128)(2,1)} %copy-done.8) | copy-start | bytes 3145732
  50.7 2.2 %collective-permute-start.4 = (bf16[640,512]{1,0:T(8,128)(2,1)S(1)}, bf16[640,512]{1,0:T(8,128)(2,1)S(1)}, u32[]{:S(2)}, u32[]{:S(2)}) collective-permute-start(bf16[640,512]{1,0:T(8,128)(2,1)S(1)} %get-tuple-element.33), channel_id=1, source_target_pairs={{0,1},{1,0},{2,3},{3,2},{4,5},{5,4},{6,7},{7,6},{8,9},{9,8},{10,11... | collective-permute-start | bytes 1966088 | tf_op jit(solution)/shard_map/ppermute | solution.py:636
  52.8 2.7 %collective-permute-start.7 = (bf16[2,512,512]{2,1,0:T(8,128)(2,1)S(1)}, bf16[2,512,512]{2,1,0:T(8,128)(2,1)S(1)}, u32[]{:S(2)}, u32[]{:S(2)}) collective-permute-start(bf16[2,512,512]{2,1,0:T(8,128)(2,1)S(1)} %get-tuple-element.38), channel_id=1, source_target_pairs={{0,1},{1,0},{2,3},{3,2},{4,5},{5,4},{6,7},{7,6},{8,9},{9,8},{10,11... | collective-permute-start | bytes 3145736 | tf_op jit(solution)/shard_map/ppermute | solution.py:636
  55.7 4.8 %collective-permute-start.8 = (bf16[2,256,512]{2,1,0:T(8,128)(2,1)S(1)}, bf16[2,256,512]{2,1,0:T(8,128)(2,1)S(1)}, u32[]{:S(2)}, u32[]{:S(2)}) collective-permute-start(bf16[2,256,512]{2,1,0:T(8,128)(2,1)S(1)} %add_convert_fusion.1.own), channel_id=1, source_target_pairs={{0,1},{1,0},{2,3},{3,2},{4,5},{5,4},{6,7},{7,6},{8,9},{9,8},{10,11... | collective-permute-start | bytes 1572872 | tf_op jit(solution)/shard_map/ppermute | solution.py:636
  56.8 13.6 %collective-permute-start.5 = (bf16[2,256,512]{2,1,0:T(8,128)(2,1)}, bf16[2,256,512]{2,1,0:T(8,128)(2,1)}, u32[]{:S(2)}, u32[]{:S(2)}) collective-permute-start(bf16[2,256,512]{2,1,0:T(8,128)(2,1)} %fusion), channel_id=1, source_target_pairs={{0,4},{4,8},{8,12},{12,16},{16,20},{20,24},{24,28},{1,5},{5,9},{9,... | collective-permute-start | bytes 1572872 | tf_op jit(solution)/shard_map/ppermute | solution.py:642
  59.0 6.7 %collective-permute-start.6 = (bf16[128,512]{1,0:T(8,128)(2,1)S(1)}, bf16[128,512]{1,0:T(8,128)(2,1)S(1)}, u32[]{:S(2)}, u32[]{:S(2)}) collective-permute-start(bf16[128,512]{1,0:T(8,128)(2,1)S(1)} %add_convert_fusion.4), channel_id=1, source_target_pairs={{0,16},{4,20},{8,24},{12,28},{16,0},{20,4},{24,8},{28,12},{1,17},{... | collective-permute-start | bytes 393224 | tf_op jit(solution)/shard_map/ppermute | solution.py:636
  70.4 11.5 %collective-permute-start.11 = (bf16[128,512]{1,0:T(8,128)(2,1)S(1)}, bf16[128,512]{1,0:T(8,128)(2,1)S(1)}, u32[]{:S(2)}, u32[]{:S(2)}) collective-permute-start(bf16[128,512]{1,0:T(8,128)(2,1)S(1)} %add_convert_fusion.3), channel_id=1, source_target_pairs={{0,12},{4,8},{8,4},{12,0},{16,28},{20,24},{24,20},{28,16},{1,13},{... | collective-permute-start | bytes 393224 | tf_op jit(solution)/shard_map/ppermute | solution.py:636
  77.1 9.3 %collective-permute-start.10 = (bf16[128,512]{1,0:T(8,128)(2,1)S(1)}, bf16[128,512]{1,0:T(8,128)(2,1)S(1)}, u32[]{:S(2)}, u32[]{:S(2)}) collective-permute-start(bf16[128,512]{1,0:T(8,128)(2,1)S(1)} %add_convert_fusion.3), channel_id=1, source_target_pairs={{0,8},{4,12},{8,0},{12,4},{16,24},{20,28},{24,16},{28,20},{1,9},{5... | collective-permute-start | bytes 393224 | tf_op jit(solution)/shard_map/ppermute | solution.py:636
  80.6 5.7 %collective-permute-start.9 = (bf16[128,512]{1,0:T(8,128)(2,1)S(1)}, bf16[128,512]{1,0:T(8,128)(2,1)S(1)}, u32[]{:S(2)}, u32[]{:S(2)}) collective-permute-start(bf16[128,512]{1,0:T(8,128)(2,1)S(1)} %add_convert_fusion.3), channel_id=1, source_target_pairs={{0,4},{4,0},{8,12},{12,8},{16,20},{20,16},{24,28},{28,24},{1,5},{5... | collective-permute-start | bytes 393224 | tf_op jit(solution)/shard_map/ppermute | solution.py:636
  81.9 4.7 %collective-permute-start.13 = (bf16[2,256,512]{2,1,0:T(8,128)(2,1)S(1)}, bf16[2,256,512]{2,1,0:T(8,128)(2,1)S(1)}, u32[]{:S(2)}, u32[]{:S(2)}) collective-permute-start(bf16[2,256,512]{2,1,0:T(8,128)(2,1)S(1)} %add_convert_fusion.own), channel_id=1, source_target_pairs={{0,1},{1,0},{2,3},{3,2},{4,5},{5,4},{6,7},{7,6},{8,9},{9,8},{10,11... | collective-permute-start | bytes 1572872 | tf_op jit(solution)/shard_map/ppermute | solution.py:636
  86.5 2.1 %collective-permute-start.12 = (bf16[128,512]{1,0:T(8,128)(2,1)S(1)}, bf16[128,512]{1,0:T(8,128)(2,1)S(1)}, u32[]{:S(2)}, u32[]{:S(2)}) collective-permute-start(bf16[128,512]{1,0:T(8,128)(2,1)S(1)} %add_convert_fusion.2), channel_id=1, source_target_pairs={{0,1},{1,0},{2,3},{3,2},{4,5},{5,4},{6,7},{7,6},{8,9},{9,8},{10,11... | collective-permute-start | bytes 393224 | tf_op jit(solution)/shard_map/ppermute | solution.py:636
